TPU v7x, 128 devices: a whole 4x4x4 slice. The times are simulated.
128 devices in a mesh: dp: 8 (over y, core), group: 16 (over x, z).
Axes of the slice: x: 4, y: 4, z: 4, core: 2. Of those that a mesh axis runs over, the one named last changes fastest.
Arguments:
- tile_maps: bfloat16 [1024, 16, 16, 384], P(('dp', 'group')), may hold values from -45 to 45
- positions: int32 [2, 1024], P(None, ('dp', 'group')), may hold values from 0 to 511
- counts: int32 [8], P('dp'), may hold values from 1 to 128, as said below
- routing: int32 [8, 16, 8], P(None, 'group'), may hold values from -1 to 31, as said below
- depth_kernel: float32 [49, 384], replicated, may hold values from -0.875 to 0.875
- depth_bias: float32 [384], replicated, may hold values from -3 to 3
- norm_gain: float32 [384], replicated, may hold values from 0.25 to 1.75
- norm_shift: float32 [384], replicated, may hold values from -2 to 2
- expand_weight: bfloat16 [384, 1536], replicated, may hold values from -0.3125 to 0.3125
- expand_bias: float32 [1536], replicated, may hold values from -1.15 to -0.75
- reduce_weight: bfloat16 [1536, 384], replicated, may hold values from -0.15625 to 0.15625
- reduce_bias: float32 [384], replicated, may hold values from -2 to 2
- layer_scale: float32 [384], replicated, may hold values from 0.3 to 1.5
- head_weight: bfloat16 [384, 768], replicated, may hold values from -0.3125 to 0.3125
- slide_taps: float32 [7, 768], replicated, may hold values from -2.5 to 2.5
- slide_weight: bfloat16 [768, 768], replicated, may hold values from -0.21875 to 0.21875
- slide_bias: float32 [768], replicated, may hold values from -2 to 2
- cotangent: float32 [8, 768], P('dp'), may hold values from -180 to 180
Outputs:
- tile_out: bfloat16 [512, 16, 16, 384], P(('dp', 'group'))
- slide_feature: float32 [8, 768], P('dp')
- grad_expand: float32 [589824], P(('dp', 'group'))
- grad_reduce: float32 [589824], P(('dp', 'group'))
- grad_depth: float32 [18816], P(('dp', 'group'))
Inputs may be any that keep to these rules, and one draw needn't show every extreme that they name: counts[d] is the number of tiles of slide d. At each group index the present tiles of all slides number at most 32, at group index 0 exactly that. routing[d, g, s] is -1 where the slot holds no tile, else e * 4 + p: the tile is processed at slot p of the device with dp index e and group index g. Each processing slot receives at most one tile; at group index 0 every one receives a tile. A device sends at most 1 tiles to each dp index, and some device sends exactly 1 to each.
All inputs are finite; a program needn't handle non-finite values.
Results may differ from a plain program's by a relative error of at most 0.013.
Values may be sent and summed in bfloat16 or wider, within the bound.
A program may use at most 128 MiB of HBM per device.

v0:
```python
import math
import jax
import jax.numpy as jnp
from jax import lax
from jax.sharding import PartitionSpec as P

E = 768
KS = 7
KERNEL_TAPS = 7
TILE_DILATION = 3
PROC = 4
EPSILON = 1e-06
HALF_ROOT = 0.7071067811865476
INV_ROOT_TAU = 0.3989422804014327


def gelu_exact(values):
    return 0.5 * values * (1.0 + jax.scipy.special.erf(values * HALF_ROOT))


def gelu_slope(values):
    return 0.5 * (
        1.0 + jax.scipy.special.erf(values * HALF_ROOT)
    ) + values * INV_ROOT_TAU * jnp.exp(-0.5 * values * values)


def contract_rows(left_side, right_side):
    return lax.dot_general(
        left_side, right_side, (((0,), (0,)), ((), ())), preferred_element_type=jnp.float32
    )


def contract_cols(left_side, right_side):
    return lax.dot_general(
        left_side, right_side, (((1,), (1,)), ((), ())), preferred_element_type=jnp.float32
    )


def padded_tiles(work_tiles):
    border_width = KS // 2
    return jnp.pad(
        work_tiles, ((0, 0), (border_width, border_width), (border_width, border_width), (0, 0))
    )


def block_forward(
    work_tiles,
    depth_kernel,
    depth_bias,
    norm_gain,
    norm_shift,
    expand_weight,
    expand_bias,
    reduce_weight,
    reduce_bias,
    layer_scale,
    head_weight,
):
    tile_count = work_tiles.shape[0]
    tile_side = work_tiles.shape[1]
    channels = work_tiles.shape[3]
    pixels = tile_side * tile_side
    padded = padded_tiles(work_tiles)
    running = jnp.zeros(work_tiles.shape, jnp.float32) + depth_bias
    for tap_row in range(KS):
        for tap_col in range(KS):
            running = (
                running
                + depth_kernel[tap_row * KS + tap_col]
                * padded[:, tap_row : tap_row + tile_side, tap_col : tap_col + tile_side]
            )
    depth_out = running.reshape(tile_count * pixels, channels)
    chan_mean = jnp.mean(depth_out, axis=1, keepdims=True)
    centred = depth_out - chan_mean
    inv_std = lax.rsqrt(jnp.mean(centred * centred, axis=1, keepdims=True) + EPSILON)
    unit_norm = centred * inv_std
    normed = (unit_norm * norm_gain + norm_shift).astype(jnp.bfloat16)
    pre_act = jnp.dot(normed, expand_weight, preferred_element_type=jnp.float32) + expand_bias
    hidden = gelu_exact(pre_act).astype(jnp.bfloat16)
    mlp_out = jnp.dot(hidden, reduce_weight, preferred_element_type=jnp.float32) + reduce_bias
    section_rows = (
        work_tiles.reshape(tile_count * pixels, channels) + layer_scale * mlp_out
    ).astype(jnp.bfloat16)
    head_pre = jnp.dot(section_rows, head_weight, preferred_element_type=jnp.float32)
    tile_embed = jnp.mean(gelu_exact(head_pre).reshape(tile_count, pixels, -1), axis=1).astype(
        jnp.bfloat16
    )
    return (
        section_rows.reshape(work_tiles.shape),
        tile_embed,
        (unit_norm, inv_std, normed, pre_act, hidden, head_pre),
    )


def block_backward(
    work_tiles,
    saved_acts,
    embed_grad,
    norm_gain,
    expand_weight,
    reduce_weight,
    layer_scale,
    head_weight,
):
    unit_norm, inv_std, normed, pre_act, hidden, head_pre = saved_acts
    tile_count = work_tiles.shape[0]
    tile_side = work_tiles.shape[1]
    channels = work_tiles.shape[3]
    pixels = tile_side * tile_side
    slope_head = gelu_slope(head_pre).reshape(tile_count, pixels, -1)
    grad_head = (embed_grad.astype(jnp.float32)[:, None, :] / float(pixels) * slope_head).astype(
        jnp.bfloat16
    )
    grad_head = grad_head.reshape(tile_count * pixels, -1)
    grad_block = contract_cols(grad_head, head_weight)
    grad_mlp = (layer_scale * grad_block).astype(jnp.bfloat16)
    reduce_grad = contract_rows(hidden, grad_mlp)
    grad_hidden = contract_cols(grad_mlp, reduce_weight)
    grad_pre = (grad_hidden * gelu_slope(pre_act)).astype(jnp.bfloat16)
    expand_grad = contract_rows(normed, grad_pre)
    grad_norm = contract_cols(grad_pre, expand_weight)
    scaled_grad = grad_norm * norm_gain
    grad_depthwise = inv_std * (
        scaled_grad
        - jnp.mean(scaled_grad, axis=1, keepdims=True)
        - unit_norm * jnp.mean(scaled_grad * unit_norm, axis=1, keepdims=True)
    )
    grad_depthwise = grad_depthwise.reshape(tile_count, tile_side, tile_side, channels)
    padded = padded_tiles(work_tiles)
    tap_grads = []
    for tap_row in range(KS):
        for tap_col in range(KS):
            tap_grads.append(
                jnp.sum(
                    grad_depthwise
                    * padded[:, tap_row : tap_row + tile_side, tap_col : tap_col + tile_side],
                    axis=(0, 1, 2),
                )
            )
    return (expand_grad, reduce_grad, jnp.stack(tap_grads))


def position_code(positions):
    half_width = E // 2
    channel_ids = jnp.arange(half_width, dtype=jnp.int32)
    frequency = jnp.exp(
        (2 * (channel_ids // 2)).astype(jnp.float32) * (-math.log(10000.0) / half_width)
    )
    pieces = []
    for coord_axis in range(2):
        angles = positions[coord_axis].astype(jnp.float32)[:, None] * frequency[None, :]
        pieces.append(jnp.where(channel_ids % 2 == 0, jnp.sin(angles), jnp.cos(angles)))
    return jnp.concatenate(pieces, axis=1)


def dilate(seq_float, slide_taps, travel_direction):
    length = seq_float.shape[0]
    border_width = KERNEL_TAPS // 2 * TILE_DILATION
    padded = jnp.pad(seq_float, ((border_width, border_width), (0, 0)))
    running = jnp.zeros(seq_float.shape, jnp.float32)
    for shift_amount in range(KERNEL_TAPS):
        leading_row = (
            border_width + travel_direction * (shift_amount - KERNEL_TAPS // 2) * TILE_DILATION
        )
        running = running + slide_taps[shift_amount] * padded[leading_row : leading_row + length]
    return running


def slide_pass(sequence, seq_present, slide_count, slide_cot, slide_taps, slide_weight, slide_bias):
    seq_float = sequence.astype(jnp.float32)
    mixed = (seq_float + dilate(seq_float, slide_taps, 1)).astype(jnp.bfloat16)
    agg_pre = jnp.dot(mixed, slide_weight, preferred_element_type=jnp.float32) + slide_bias
    weight = seq_present.astype(jnp.float32) / slide_count.astype(jnp.float32)
    feature = jnp.sum(gelu_exact(agg_pre) * weight[:, None], axis=0)
    grad_agg = (slide_cot[None, :] * weight[:, None] * gelu_slope(agg_pre)).astype(jnp.bfloat16)
    grad_mixed = contract_cols(grad_agg, slide_weight)
    seq_grad = (
        (grad_mixed + dilate(grad_mixed, slide_taps, -1)) * seq_present.astype(jnp.float32)[:, None]
    ).astype(jnp.bfloat16)
    return (feature, seq_grad)


def sender_table(my_list, slides, places):
    dest_dev = jnp.where(my_list >= 0, my_list // PROC, -1)
    is_hit = dest_dev[None, :] == jnp.arange(slides, dtype=jnp.int32)[:, None]
    order_rank = jnp.cumsum(is_hit.astype(jnp.int32), axis=1) - 1
    chosen = is_hit[:, None, :] & (
        order_rank[:, None, :] == jnp.arange(places, dtype=jnp.int32)[None, :, None]
    )
    return chosen.reshape(slides * places, -1)


def receiver_table(route_rows, my_slide, places):
    dest_dev = jnp.where(route_rows >= 0, route_rows // PROC, -1)
    is_hit = dest_dev == my_slide
    order_rank = jnp.cumsum(is_hit.astype(jnp.int32), axis=1) - 1
    chosen = is_hit[:, None, :] & (
        order_rank[:, None, :] == jnp.arange(places, dtype=jnp.int32)[None, :, None]
    )
    target = jnp.sum(jnp.where(chosen, (route_rows % PROC)[:, None, :], 0), axis=2).reshape(-1)
    is_used = jnp.any(chosen, axis=2).reshape(-1)
    return (target[None, :] == jnp.arange(PROC, dtype=jnp.int32)[:, None]) & is_used[None, :]


def on_device(
    tile_maps,
    positions,
    counts,
    routing,
    depth_kernel,
    depth_bias,
    norm_gain,
    norm_shift,
    expand_weight,
    expand_bias,
    reduce_weight,
    reduce_bias,
    layer_scale,
    head_weight,
    slide_taps,
    slide_weight,
    slide_bias,
    cotangent,
):
    params = (
        depth_kernel,
        depth_bias,
        norm_gain,
        norm_shift,
        expand_weight,
        expand_bias,
        reduce_weight,
        reduce_bias,
        layer_scale,
        head_weight,
    )
    slides = lax.axis_size("dp")
    members = lax.axis_size("group")
    my_slide = lax.axis_index("dp")
    my_member = lax.axis_index("group")
    slot_count = tile_maps.shape[0]
    embed_width = head_weight.shape[1]
    places = slot_count // slides
    route_rows = routing[:, 0, :]
    my_list = lax.dynamic_index_in_dim(route_rows, my_slide, 0, keepdims=False)
    send_pick = sender_table(my_list, slides, places).astype(jnp.bfloat16)
    take_bool = receiver_table(route_rows, my_slide, places)
    take_pick = take_bool.astype(jnp.bfloat16)
    filled = jnp.any(take_bool, axis=1)
    packed = jnp.dot(
        send_pick, tile_maps.reshape(slot_count, -1), preferred_element_type=jnp.float32
    ).astype(jnp.bfloat16)
    packed = packed.reshape((slides * places,) + tile_maps.shape[1:])
    arrived = lax.all_to_all(packed, "dp", split_axis=0, concat_axis=0, tiled=True)
    work_tiles = jnp.dot(
        take_pick, arrived.reshape(slides * places, -1), preferred_element_type=jnp.float32
    ).astype(jnp.bfloat16)
    work_tiles = work_tiles.reshape((take_pick.shape[0],) + tile_maps.shape[1:])
    section_out, tile_embed, saved_acts = block_forward(work_tiles, *params)
    tile_out = jnp.where(filled[:, None, None, None], section_out, jnp.zeros((), jnp.bfloat16))
    returned = contract_rows(take_pick, tile_embed).astype(jnp.bfloat16)
    came_back = lax.all_to_all(returned, "dp", split_axis=0, concat_axis=0, tiled=True)
    own_emb = contract_rows(send_pick, came_back)
    slide_count = counts[0]
    own_seq = jnp.arange(slot_count, dtype=jnp.int32) * members + my_member
    own_present = own_seq < slide_count
    slide_rows = jnp.where(
        own_present[:, None],
        (own_emb + position_code(positions)).astype(jnp.bfloat16),
        jnp.zeros((), jnp.bfloat16),
    )
    gathered = lax.all_gather(
        slide_rows.reshape(slot_count, 1, embed_width), "group", axis=1, tiled=True
    )
    sequence = gathered.reshape(slot_count * members, embed_width)
    seq_present = jnp.arange(slot_count * members, dtype=jnp.int32) < slide_count
    slide_cot = cotangent[0]
    feature, seq_grad = slide_pass(
        sequence, seq_present, slide_count, slide_cot, slide_taps, slide_weight, slide_bias
    )
    own_grad = lax.dynamic_index_in_dim(
        seq_grad.reshape(slot_count, members, embed_width), my_member, 1, keepdims=False
    )
    outgoing = jnp.dot(send_pick, own_grad, preferred_element_type=jnp.float32).astype(jnp.bfloat16)
    incoming = lax.all_to_all(outgoing, "dp", split_axis=0, concat_axis=0, tiled=True)
    embed_grad = jnp.dot(take_pick, incoming, preferred_element_type=jnp.float32).astype(
        jnp.bfloat16
    )
    source_tiles, _ = lax.optimization_barrier((work_tiles, embed_grad))
    kept_acts = block_forward(source_tiles, *params)[2]
    expand_grad, reduce_grad, depth_grad = block_backward(
        source_tiles,
        kept_acts,
        embed_grad,
        norm_gain,
        expand_weight,
        reduce_weight,
        layer_scale,
        head_weight,
    )
    shares = (
        lax.psum_scatter(expand_grad.reshape(-1), ("dp", "group"), scatter_dimension=0, tiled=True),
        lax.psum_scatter(reduce_grad.reshape(-1), ("dp", "group"), scatter_dimension=0, tiled=True),
        lax.psum_scatter(depth_grad.reshape(-1), ("dp", "group"), scatter_dimension=0, tiled=True),
    )
    return (tile_out, feature[None, :], shares[0], shares[1], shares[2])


def solution(mesh):
    return jax.shard_map(
        on_device,
        mesh=mesh,
        in_specs=(
            P(("dp", "group"), None, None, None),
            P(None, ("dp", "group")),
            P("dp"),
            P(None, "group", None),
            P(),
            P(),
            P(),
            P(),
            P(),
            P(),
            P(),
            P(),
            P(),
            P(),
            P(),
            P(),
            P(),
            P("dp", None),
        ),
        out_specs=(
            P(("dp", "group"), None, None, None),
            P("dp", None),
            P(("dp", "group")),
            P(("dp", "group")),
            P(("dp", "group")),
        ),
        check_vma=False,
    )
```

profile of v0, /device:TPU:1, one launch (start us, length us, event | category | flops | bytes accessed | tf_op | source)
XLA Modules:
  0.0 371.2 jit_solution(15879071314645622072)
XLA Ops:
  7.2 0.8 compare_select_fusion.4
  8.1 2.3 copy.39
  11.0 1.4 copy.32
  12.4 6.1 %all-to-all-start = ((bf16[8,16,16,384]{3,2,1,0:T(8,128)(2,1)}), bf16[8,16,16,384]{3,2,1,0:T(8,128)(2,1)S(1)}, u32[]{:S(2)}, u32[]{:S(2)}) async-start(bf16[8,16,16,384]{3,2,1,0:T(8,128)(2,1)} %copy.32), calls=%async_computation | async-start | bytes 3145728 | tf_op jit(solution)/shard_map/all_to_all | solution.py:254
  18.6 1.4 reduce_window_sum.17
  23.6 0.7 slice_reduce_fusion.54
  24.3 0.7 slice_reduce_fusion.55
  25.6 0.8 fusion.166
  26.4 12.8 %all-to-all-done = bf16[8,16,16,384]{3,2,1,0:T(8,128)(2,1)S(1)} async-done(((bf16[8,16,16,384]{3,2,1,0:T(8,128)(2,1)}), bf16[8,16,16,384]{3,2,1,0:T(8,128)(2,1)S(1)}, u32[]{:S(2)}, u32[]{:S(2)}) %all-to-all-start) | async-done | bytes 1572896 | tf_op jit(solution)/shard_map/all_to_all | solution.py:254
  39.2 0.9 copy.40
  40.7 1.6 reshape.395
  43.3 12.8 %fusion.203 = (f32[4,16,16]{2,1,0:T(8,128)S(1)}, f32[4,16,16,384]{3,2,1,0:T(8,128)S(1)}) fusion(f32[384]{0:T(512)S(1)} %copy-done.11, f32[384]{0:T(512)S(1)} %copy-done.12, f32[384]{0:T(512)S(1)} %copy-done.33, f32[384]{0:T(512)S(1)} %copy-done.34, f32[384]{0:T(512)S(1)} %copy-done.35, f32[384]{0:T(512)S(1)} %copy-done.36, f32[384]{0:T(512)S(1)} %copy-done.37, ...), kind=kLoop, calls=%fused_computation.532 | loop fusion | flops 58194944 | bytes 2440192 | tf_op jit(solution)/shard_map/reduce_sum | solution.py:73
  56.8 1.4 div.79
  58.2 1.1 multiply_reduce_fusion.3
  60.0 1.4 rsqrt.23
  61.4 1.9 fusion.112
  63.4 5.5 %add_convert_fusion.1 = bf16[1024,384]{1,0:T(8,128)(2,1)S(1)} fusion(f32[1024,384]{1,0:T(8,128)} %reshape.395, bf16[1536,384]{1,0:T(8,128)(2,1)} %param.28, bf16[1024,384]{1,0:T(8,128)(2,1)} %fusion.112, bf16[384,1536]{1,0:T(8,128)(2,1)S(1)} %copy-done, f32[1536]{0:T(1024)} %param.27, f32[384]{0:T(512)} %param.29, f32[384]{0:T(512)} %param.30), kind=kOutput, calls=%fused_computation.323 | convolution fusion | flops 2426929152 | bytes 5514240 | tf_op jit(solution)/shard_map/dot_general | solution.py:80
  69.1 1.3 bitcast_reduce_fusion
  72.4 4.1 %all-to-all-start.1 = ((bf16[8,2,384]{2,1,0:T(2,128)(2,1)}), bf16[8,2,384]{2,1,0:T(2,128)(2,1)S(1)}, u32[]{:S(2)}, u32[]{:S(2)}) async-start(bf16[8,2,384]{2,1,0:T(2,128)(2,1)} %reshape.458), calls=%async_computation.1 | async-start | bytes 24576 | tf_op jit(solution)/shard_map/all_to_all | solution.py:262
  76.6 4.6 %all-to-all-done.1 = bf16[8,2,384]{2,1,0:T(2,128)(2,1)S(1)} async-done(((bf16[8,2,384]{2,1,0:T(2,128)(2,1)}), bf16[8,2,384]{2,1,0:T(2,128)(2,1)S(1)}, u32[]{:S(2)}, u32[]{:S(2)}) %all-to-all-start.1) | async-done | bytes 12320 | tf_op jit(solution)/shard_map/all_to_all | solution.py:262
  81.4 19.9 %all-gather = bf16[8,12288]{1,0:T(8,128)(2,1)S(1)} all-gather(bf16[8,768]{1,0:T(8,128)(2,1)S(1)} %fusion.116), channel_id=2, replica_groups=mesh['dp'=8,'group'=16] {'group'}, dimensions={1}, use_global_device_ids=true | all-gather | bytes 208896 | tf_op jit(solution)/shard_map/all_gather | solution.py:272
  101.4 2.6 multiply_reduce_fusion.4
  105.8 12.9 %all_to_all.29 = bf16[8,2,384]{2,1,0:T(2,128)(2,1)S(1)} all-to-all(bf16[8,2,384]{2,1,0:T(2,128)(2,1)S(1)} %reshape.460), channel_id=1, replica_groups=mesh['dp'=8,'group'=16] {'dp'}, dimensions={0} | all-to-all | bytes 24576 | tf_op jit(solution)/shard_map/all_to_all | solution.py:285
  118.7 0.7 convert_multiply_fusion.96
  119.5 13.6 %fusion.199 = (f32[4,16,16]{2,1,0:T(8,128)S(1)}, f32[4,16,16,384]{3,2,1,0:T(8,128)S(1)}) fusion(f32[384]{0:T(512)} %get-tuple-element.105, f32[384]{0:T(512)} %get-tuple-element.106, f32[384]{0:T(512)} %get-tuple-element.59, f32[384]{0:T(512)} %get-tuple-element.60, f32[384]{0:T(512)} %get-tuple-element.61, f32[384]{0:T(512)} %get-tuple-element.62, ...), kind=kLoop, calls=%fused_computation.530 | loop fusion | flops 58194944 | bytes 2440192 | tf_op jit(solution)/shard_map/reduce_sum | solution.py:73
  133.7 0.8 div.87
  134.6 1.1 multiply_reduce_fusion.2
  136.3 0.8 rsqrt.25
  137.9 2.7 multiply_convert_fusion
  140.6 1.8 fusion.107
  142.5 1.8 fusion.9
  144.3 1.0 multiply_convert_fusion.2
  145.3 3.3 fusion.206
  148.6 3.5 fusion.4
  152.0 2.9 fusion.205
  154.9 2.0 fusion.198
  156.9 6.2 %fusion.105 = (f32[384]{0:T(512)S(1)}, f32[384]{0:T(512)}, f32[384]{0:T(512)}, f32[384]{0:T(512)}, f32[384]{0:T(512)}, /*index=5*/f32[384]{0:T(512)}, f32[384]{0...) fusion(bf16[4,16,16,384]{3,2,1,0:T(8,128)(2,1)S(1)} %bitcast.16, ...), kind=kLoop, calls=%fused_computation.306 | loop fusion | flops 23586048 | bytes 5549056 | tf_op jit(solution)/shard_map/reduce_sum | solution.py:134
  163.1 3.2 fusion.104
  166.3 4.4 %fusion.106 = (f32[384]{0:T(512)}, f32[384]{0:T(512)}, f32[384]{0:T(512)}, f32[384]{0:T(512)}, f32[384]{0:T(512)}, /*index=5*/f32[384]{0:T(512)}, f32[384]{0:T(5...) fusion(bf16[4,16,16,384]{3,2,1,0:T(8,128)(2,1)S(1)} %bitcast.16, ...), kind=kLoop, calls=%fused_computation.307 | loop fusion | flops 21226752 | bytes 2386944 | tf_op jit(solution)/shard_map/reduce_sum | solution.py:134
  170.7 3.3 reshape.391
  174.0 1.5 reshape.392
  189.7 0.7 stack.171
  206.7 1.1 copy-done.3
  207.8 1.0 broadcast_select_fusion
  209.4 150.8 %all-reduce.10.cloned.1.call-done = (f32[589824]{0:T(1024)}, f32[589824]{0:T(1024)}, f32[18816]{0:T(1024)}) async-done(((f32[589824]{0:T(1024)}, f32[589824]{0:T(1024)}, f32[18816]{0:T(1024)}), (f32[589824]{0:T(1024)}, f32[589824]{0:T(1024)}, f32[18816]{0:T(1024)})) %all-reduce.10.cloned.1.call-update) | async-done | bytes 4793872
  360.2 1.4 dynamic-slice.1
  361.6 1.4 dynamic-slice.2
  363.0 1.3 dynamic-slice.3
  (247 shorter events, 43.9 us)
Async XLA Ops:
  7.2 56.2 %copy-start = (bf16[384,1536]{1,0:T(8,128)(2,1)S(1)}, bf16[384,1536]{1,0:T(8,128)(2,1)}, u32[]{:S(2)}) copy-start(bf16[384,1536]{1,0:T(8,128)(2,1)} %param.26) | copy-start | bytes 3538948
  8.1 2.3 copy-start.55
  12.4 6.1 %copy-start.64 = (s32[8,1,8]{2,1,0:T(1,128)S(1)}, s32[8,1,8]{2,1,0:T(1,128)}, u32[]{:S(2)}) copy-start(s32[8,1,8]{2,1,0:T(1,128)} %param.21) | copy-start | bytes 772
  12.4 9.9 %copy-start.4 = (f32[49,384]{1,0:T(8,128)S(1)}, f32[49,384]{1,0:T(8,128)}, u32[]{:S(2)}) copy-start(f32[49,384]{1,0:T(8,128)} %param.22) | copy-start | bytes 225796
  12.4 10.5 %copy-start.5 = (f32[7,768]{1,0:T(8,128)S(1)}, f32[7,768]{1,0:T(8,128)}, u32[]{:S(2)}) copy-start(f32[7,768]{1,0:T(8,128)} %param.32) | copy-start | bytes 64516
  12.4 13.2 %copy-start.67 = (s32[2,8]{1,0:T(2,128)S(1)}, s32[2,8]{1,0:T(2,128)}, u32[]{:S(2)}) copy-start(s32[2,8]{1,0:T(2,128)} %param.19) | copy-start | bytes 196
  12.4 26.8 %all-to-all-start = ((bf16[8,16,16,384]{3,2,1,0:T(8,128)(2,1)}), bf16[8,16,16,384]{3,2,1,0:T(8,128)(2,1)S(1)}, u32[]{:S(2)}, u32[]{:S(2)}) async-start(bf16[8,16,16,384]{3,2,1,0:T(8,128)(2,1)} %copy.32), calls=%async_computation | async-start | bytes 3145728 | tf_op jit(solution)/shard_map/all_to_all | solution.py:254
  25.6 14.5 %copy-start.61 = (pred[4,8]{1,0:T(4,128)(4,1)}, pred[4,8]{1,0:T(4,128)(4,1)S(1)}, u32[]{:S(2)}) copy-start(pred[4,8]{1,0:T(4,128)(4,1)S(1)} %get-tuple-element.121) | copy-start | bytes 100
  42.3 0.7 copy-start.8
  42.3 0.7 copy-start.9
  42.3 0.7 copy-start.10
  42.4 0.7 copy-start.19
  42.5 0.7 copy-start.33
  42.6 0.7 copy-start.34
  42.6 0.7 copy-start.35
  63.4 5.5 %copy-start.71 = (bf16[384,768]{1,0:T(8,128)(2,1)S(1)}, bf16[384,768]{1,0:T(8,128)(2,1)}, u32[]{:S(2)}) copy-start(bf16[384,768]{1,0:T(8,128)(2,1)} %param.31) | copy-start | bytes 1769476
  68.9 1.5 copy-start.2
  68.9 1.5 copy-start.62
  68.9 7.6 %copy-start.65 = (f32[1,768]{1,0:T(1,128)S(1)}, f32[1,768]{1,0:T(1,128)}, u32[]{:S(2)}) copy-start(f32[1,768]{1,0:T(1,128)} %param.35) | copy-start | bytes 9220
  68.9 12.3 %copy-start.52 = (f32[8,384]{1,0:T(8,128)S(1)}, f32[8,384]{1,0:T(8,128)}, u32[]{:S(2)}) copy-start(f32[8,384]{1,0:T(8,128)} %get-tuple-element.129) | copy-start | bytes 36868
  68.9 12.3 %copy-start.53 = (f32[8,384]{1,0:T(8,128)S(1)}, f32[8,384]{1,0:T(8,128)}, u32[]{:S(2)}) copy-start(f32[8,384]{1,0:T(8,128)} %get-tuple-element.130) | copy-start | bytes 36868
  69.0 12.3 %copy-start.56 = (pred[8,8]{1,0:T(8,128)(4,1)S(1)}, pred[8,8]{1,0:T(8,128)(4,1)}, u32[]{:S(2)}) copy-start(pred[8,8]{1,0:T(8,128)(4,1)} %copy-done.55) | copy-start | bytes 196
  69.0 32.4 %copy-start.45 = (f32[768]{0:T(1024)S(1)}, f32[768]{0:T(1024)}, u32[]{:S(2)}) copy-start(f32[768]{0:T(1024)} %get-tuple-element.107) | copy-start | bytes 9220
  69.0 32.4 %copy-start.46 = (f32[768]{0:T(1024)S(1)}, f32[768]{0:T(1024)}, u32[]{:S(2)}) copy-start(f32[768]{0:T(1024)} %get-tuple-element.108) | copy-start | bytes 9220
  69.0 32.4 %copy-start.47 = (f32[768]{0:T(1024)S(1)}, f32[768]{0:T(1024)}, u32[]{:S(2)}) copy-start(f32[768]{0:T(1024)} %get-tuple-element.109) | copy-start | bytes 9220
  69.0 32.4 %copy-start.48 = (f32[768]{0:T(1024)S(1)}, f32[768]{0:T(1024)}, u32[]{:S(2)}) copy-start(f32[768]{0:T(1024)} %get-tuple-element.110) | copy-start | bytes 9220
  69.0 32.4 %copy-start.49 = (f32[768]{0:T(1024)S(1)}, f32[768]{0:T(1024)}, u32[]{:S(2)}) copy-start(f32[768]{0:T(1024)} %get-tuple-element.111) | copy-start | bytes 9220
  69.0 32.4 %copy-start.50 = (f32[768]{0:T(1024)S(1)}, f32[768]{0:T(1024)}, u32[]{:S(2)}) copy-start(f32[768]{0:T(1024)} %get-tuple-element.112) | copy-start | bytes 9220
  69.0 32.4 %copy-start.51 = (f32[768]{0:T(1024)S(1)}, f32[768]{0:T(1024)}, u32[]{:S(2)}) copy-start(f32[768]{0:T(1024)} %get-tuple-element.113) | copy-start | bytes 9220
  69.0 32.4 %copy-start.74 = (f32[768]{0:T(1024)S(1)}, f32[768]{0:T(1024)}, u32[]{:S(2)}) copy-start(f32[768]{0:T(1024)} %param.34) | copy-start | bytes 9220
  69.0 32.4 %copy-start.77 = (f32[128]{0:T(128)S(1)}, f32[128]{0:T(128)}, u32[]{:S(2)}) copy-start(f32[128]{0:T(128)} %compare_select_fusion.8) | copy-start | bytes 1540
  72.4 8.8 %all-to-all-start.1 = ((bf16[8,2,384]{2,1,0:T(2,128)(2,1)}), bf16[8,2,384]{2,1,0:T(2,128)(2,1)S(1)}, u32[]{:S(2)}, u32[]{:S(2)}) async-start(bf16[8,2,384]{2,1,0:T(2,128)(2,1)} %reshape.458), calls=%async_computation.1 | async-start | bytes 24576 | tf_op jit(solution)/shard_map/all_to_all | solution.py:262
  76.5 283.7 %all-reduce.10.cloned.1.call-start = ((), (), s32[]{:S(2)}) async-start(), calls=%async_computation.3 | async-start | bytes 9592832
  101.4 2.6 copy-start.69
  133.1 4.1 %copy-start.57 = (f32[384]{0:T(512)S(1)}, f32[384]{0:T(512)}, u32[]{:S(2)}) copy-start(f32[384]{0:T(512)} %param.25) | copy-start | bytes 4612
  133.1 4.0 %copy-start.58 = (f32[384]{0:T(512)S(1)}, f32[384]{0:T(512)}, u32[]{:S(2)}) copy-start(f32[384]{0:T(512)} %param.24) | copy-start | bytes 4612
  137.2 0.7 copy-start.73
  137.9 2.7 copy-start.70
  137.9 2.7 copy-start.75
  137.9 2.7 copy-start.76
  140.6 1.9 copy-start.54
  140.6 1.9 copy-start.72
  170.7 3.3 copy-start.1
  174.0 23.1 %copy-start.60 = (f32[384]{0:T(512)S(1)}, f32[384]{0:T(512)}, u32[]{:S(2)}) copy-start(f32[384]{0:T(512)} %get-tuple-element.40) | copy-start | bytes 4612
  174.0 23.1 %copy-start.59 = (f32[384]{0:T(512)S(1)}, f32[384]{0:T(512)}, u32[]{:S(2)}) copy-start(f32[384]{0:T(512)} %get-tuple-element.41) | copy-start | bytes 4612
  206.7 1.1 copy-start.3
  206.7 1.1 copy-start.66
  206.7 2.1 copy-start.63
  (33 other events, 22.4 us)
Sparse Core Ops, SparseCore 0:
  206.8 153.3 all-reduce.9
where the time goes:
time: 373 us; the launch traced here: 371 us
  waiting for transfers between devices  168 us (45%)
  local copies, waits for them, and re-layouts  57.7 us (15%)
  other arithmetic  55.4 us (15%)
  blocking collectives  32.8 us (9%)
  matrix products  31.1 us (8%)
  between operations  15.8 us (4%)
  starting transfers between devices  10.2 us (3%)
    unnamed x2, waiting for transfers between devices  151 us
    another operation x50, local copies, waits for them, and re-layouts, block_backward(): return (expand_grad, reduce_grad, jnp.stack(tap_grads))  30.5 us
    reduce_sum x2, other arithmetic, block_forward(): chan_mean = jnp.mean(depth_out, axis=1, keepdims=True)  26.4 us
    all_gather x1, blocking collectives, on_device(): lax.all_gather(slide_rows.reshape(slot_count, 1, embed_width), 'group', a...  19.9 us
    reduce_sum x3, other arithmetic, block_backward(): jnp.sum(grad_depthwise * padded[:, tap_row:tap_row + tile_side, tap_col:t...  13.8 us
    all_to_all x1, blocking collectives, on_device(): lax.all_to_all(outgoing, 'dp', split_axis=0, concat_axis=0, tiled=True)  12.9 us
    all_to_all x1, waiting for transfers between devices, on_device(): lax.all_to_all(packed, 'dp', split_axis=0, concat_axis=0, tiled=True)  12.8 us
    unnamed x166, local copies, waits for them, and re-layouts  10.3 us
  transfers between devices with their start and end apart: 3, of which 3 were waited for; matrix products, arithmetic and copies ran while one was open for 2% of the time, Pallas kernels for 0%

commit v1 on v0

--- a/solution.py
+++ b/solution.py
@@ -269,9 +269,9 @@
         (own_emb + position_code(positions)).astype(jnp.bfloat16),
         jnp.zeros((), jnp.bfloat16),
     )
-    gathered = lax.all_gather(
-        slide_rows.reshape(slot_count, 1, embed_width), "group", axis=1, tiled=True
-    )
+    block = slide_rows.reshape(slot_count, 1, embed_width)
+    sent = jnp.stack([block] * lax.axis_size("group"))
+    gathered = jnp.concatenate(lax.all_to_all(sent, "group", 0, 0), axis=1)
     sequence = gathered.reshape(slot_count * members, embed_width)
     seq_present = jnp.arange(slot_count * members, dtype=jnp.int32) < slide_count
     slide_cot = cotangent[0]

time: 373 us -> 334 us (0.90)
  local copies, waits for them, and re-layouts: 57.7 us -> 29.4 us
  blocking collectives: 32.8 us -> 9.04 us
  starting transfers between devices: 10.2 us -> 17.8 us
  waiting for transfers between devices: 168 us -> 175 us
    another operation x50, local copies, waits for them, and re-layouts: 30.5 us -> 0.35 us  [block_backward(): return (expand_grad, reduce_grad, jnp.stack(tap_grads))]
    all_gather x1 -> x0, blocking collectives: 19.9 us -> none  [on_device(): lax.all_gather(slide_rows.reshape(slot_count, 1, embed_width), 'group', a...]
    all_to_all x0 -> x1, starting transfers between devices: none -> 7.59 us  [on_device(): gathered = jnp.concatenate(lax.all_to_all(sent, 'group', 0, 0), axis=1)]
    all_to_all x0 -> x1, waiting for transfers between devices: none -> 6.97 us  [on_device(): gathered = jnp.concatenate(lax.all_to_all(sent, 'group', 0, 0), axis=1)]
    all_to_all x1, blocking collectives: 12.9 us -> 9.04 us  [on_device(): lax.all_to_all(outgoing, 'dp', split_axis=0, concat_axis=0, tiled=True)]
    unnamed x166 -> x176, local copies, waits for them, and re-layouts: 10.3 us -> 10.4 us
  transfers between devices with their start and end apart: 3 -> 4, of which waited for: 3 -> 4; matrix products, arithmetic and copies ran while one was open for 2% -> 2% of each run, Pallas kernels for 0% -> 0%
where the time goes in v1:
time: 334 us; the launch traced here: 332 us
  waiting for transfers between devices  175 us (52%)
  other arithmetic  53.6 us (16%)
  matrix products  31.1 us (9%)
  local copies, waits for them, and re-layouts  29.4 us (9%)
  starting transfers between devices  17.8 us (5%)
  between operations  16.2 us (5%)
  blocking collectives  9.04 us (3%)
    unnamed x2, waiting for transfers between devices  149 us
    reduce_sum x2, other arithmetic, block_forward(): chan_mean = jnp.mean(depth_out, axis=1, keepdims=True)  26.4 us
    all_to_all x1, waiting for transfers between devices, on_device(): lax.all_to_all(packed, 'dp', split_axis=0, concat_axis=0, tiled=True)  14.1 us
    reduce_sum x3, other arithmetic, block_backward(): jnp.sum(grad_depthwise * padded[:, tap_row:tap_row + tile_side, tap_col:t...  12.6 us
    unnamed x176, local copies, waits for them, and re-layouts  10.4 us
    all_to_all x1, blocking collectives, on_device(): lax.all_to_all(outgoing, 'dp', split_axis=0, concat_axis=0, tiled=True)  9.04 us
    all_to_all x1, starting transfers between devices, on_device(): gathered = jnp.concatenate(lax.all_to_all(sent, 'group', 0, 0), axis=1)  7.59 us
    dot_general x2, matrix products, block_forward(): jnp.dot(hidden, reduce_weight, preferred_element_type=jnp.float32)  7.33 us
  transfers between devices with their start and end apart: 4, of which 4 were waited for; matrix products, arithmetic and copies ran while one was open for 2% of the time, Pallas kernels for 0%

profile of v1, /device:TPU:1, one launch (start us, length us, event | category | flops | bytes accessed | tf_op | source)
XLA Modules:
  0.0 332.3 jit_solution(16169847744508133097)
XLA Ops:
  7.2 0.8 compare_select_fusion.4
  8.1 2.3 copy.42
  11.0 1.4 copy.34
  12.4 6.1 %all-to-all-start = ((bf16[8,16,16,384]{3,2,1,0:T(8,128)(2,1)}), bf16[8,16,16,384]{3,2,1,0:T(8,128)(2,1)S(1)}, u32[]{:S(2)}, u32[]{:S(2)}) async-start(bf16[8,16,16,384]{3,2,1,0:T(8,128)(2,1)} %copy.34), calls=%async_computation | async-start | bytes 3145728 | tf_op jit(solution)/shard_map/all_to_all | solution.py:254
  19.7 1.4 reduce_window_sum.17
  23.0 0.7 slice_reduce_fusion.55
  24.4 0.8 fusion.166
  25.1 14.1 %all-to-all-done = bf16[8,16,16,384]{3,2,1,0:T(8,128)(2,1)S(1)} async-done(((bf16[8,16,16,384]{3,2,1,0:T(8,128)(2,1)}), bf16[8,16,16,384]{3,2,1,0:T(8,128)(2,1)S(1)}, u32[]{:S(2)}, u32[]{:S(2)}) %all-to-all-start) | async-done | bytes 1572896 | tf_op jit(solution)/shard_map/all_to_all | solution.py:254
  39.2 0.9 copy.43
  40.7 1.6 reshape.393
  43.3 12.8 %fusion.203 = (f32[4,16,16]{2,1,0:T(8,128)S(1)}, f32[4,16,16,384]{3,2,1,0:T(8,128)S(1)}) fusion(f32[384]{0:T(512)S(1)} %copy-done.10, f32[384]{0:T(512)S(1)} %copy-done.11, f32[384]{0:T(512)S(1)} %copy-done.32, f32[384]{0:T(512)S(1)} %copy-done.33, f32[384]{0:T(512)S(1)} %copy-done.34, f32[384]{0:T(512)S(1)} %copy-done.35, f32[384]{0:T(512)S(1)} %copy-done.36, ...), kind=kLoop, calls=%fused_computation.533 | loop fusion | flops 58194944 | bytes 2440192 | tf_op jit(solution)/shard_map/reduce_sum | solution.py:73
  56.8 1.4 div.79
  58.2 1.1 multiply_reduce_fusion.3
  60.0 1.4 rsqrt.23
  61.4 2.0 fusion.112
  63.4 5.5 %add_convert_fusion.1 = bf16[1024,384]{1,0:T(8,128)(2,1)S(1)} fusion(f32[1024,384]{1,0:T(8,128)} %reshape.393, bf16[1536,384]{1,0:T(8,128)(2,1)} %param.28, bf16[1024,384]{1,0:T(8,128)(2,1)} %fusion.112, bf16[384,1536]{1,0:T(8,128)(2,1)S(1)} %copy-done, f32[1536]{0:T(1024)} %param.27, f32[384]{0:T(512)} %param.29, f32[384]{0:T(512)} %param.30), kind=kOutput, calls=%fused_computation.323 | convolution fusion | flops 2426929152 | bytes 5514240 | tf_op jit(solution)/shard_map/dot_general | solution.py:80
  69.0 1.3 bitcast_reduce_fusion
  72.3 4.1 %all-to-all-start.1 = ((bf16[8,2,384]{2,1,0:T(2,128)(2,1)}), bf16[8,2,384]{2,1,0:T(2,128)(2,1)S(1)}, u32[]{:S(2)}, u32[]{:S(2)}) async-start(bf16[8,2,384]{2,1,0:T(2,128)(2,1)} %reshape.453), calls=%async_computation.1 | async-start | bytes 24576 | tf_op jit(solution)/shard_map/all_to_all | solution.py:262
  76.5 4.6 %all-to-all-done.1 = bf16[8,2,384]{2,1,0:T(2,128)(2,1)S(1)} async-done(((bf16[8,2,384]{2,1,0:T(2,128)(2,1)}), bf16[8,2,384]{2,1,0:T(2,128)(2,1)S(1)}, u32[]{:S(2)}, u32[]{:S(2)}) %all-to-all-start.1) | async-done | bytes 12320 | tf_op jit(solution)/shard_map/all_to_all | solution.py:262
  81.3 0.7 stack.153
  82.0 7.6 %all-to-all-start.2 = ((bf16[16,8,1,768]{3,1,2,0:T(8,128)(2,1)}), bf16[16,8,1,768]{3,1,2,0:T(8,128)(2,1)S(1)}, u32[]{:S(2)}, u32[]{:S(2)}) async-start(bf16[16,8,1,768]{3,1,2,0:T(8,128)(2,1)} %stack.153), calls=%async_computation.2 | async-start | bytes 393216 | tf_op jit(solution)/shard_map/all_to_all | solution.py:274
  89.8 7.0 %all-to-all-done.2 = bf16[16,8,1,768]{3,1,2,0:T(8,128)(2,1)S(1)} async-done(((bf16[16,8,1,768]{3,1,2,0:T(8,128)(2,1)}), bf16[16,8,1,768]{3,1,2,0:T(8,128)(2,1)S(1)}, u32[]{:S(2)}, u32[]{:S(2)}) %all-to-all-start.2) | async-done | bytes 196640 | tf_op jit(solution)/shard_map/all_to_all | solution.py:274
  96.9 2.6 multiply_reduce_fusion.4
  101.3 9.0 %all_to_all.34 = bf16[8,2,384]{2,1,0:T(2,128)(2,1)S(1)} all-to-all(bf16[8,2,384]{2,1,0:T(2,128)(2,1)S(1)} %reshape.455), channel_id=1, replica_groups=mesh['dp'=8,'group'=16] {'dp'}, dimensions={0} | all-to-all | bytes 24576 | tf_op jit(solution)/shard_map/all_to_all | solution.py:285
  110.4 0.7 convert_multiply_fusion.96
  111.1 13.6 %fusion.199 = (f32[4,16,16]{2,1,0:T(8,128)S(1)}, f32[4,16,16,384]{3,2,1,0:T(8,128)S(1)}) fusion(f32[384]{0:T(512)} %get-tuple-element.105, f32[384]{0:T(512)} %get-tuple-element.106, f32[384]{0:T(512)} %get-tuple-element.59, f32[384]{0:T(512)} %get-tuple-element.60, f32[384]{0:T(512)} %get-tuple-element.61, f32[384]{0:T(512)} %get-tuple-element.62, ...), kind=kLoop, calls=%fused_computation.531 | loop fusion | flops 58194944 | bytes 2440192 | tf_op jit(solution)/shard_map/reduce_sum | solution.py:73
  125.4 0.8 div.87
  126.2 1.1 multiply_reduce_fusion.2
  127.9 0.8 rsqrt.25
  129.5 2.7 multiply_convert_fusion
  132.2 1.8 fusion.107
  134.1 1.8 fusion.9
  135.9 1.0 multiply_convert_fusion.2
  136.9 3.3 fusion.206
  140.2 3.4 %fusion.4 = bf16[1024,1536]{1,0:T(8,128)(2,1)S(1)} fusion(f32[1024,1536]{1,0:T(8,128)S(1)} %get-tuple-element.136, bf16[1024,384]{1,0:T(8,128)(2,1)S(1)} %multiply_convert_fusion.2, bf16[1536,384]{1,0:T(8,128)(2,1)S(1)} %copy-done.76, f32[1536]{0:T(1024)S(1)} %copy-done.79), kind=kOutput, calls=%fused_computation.103 | convolution fusion | flops 1225261056 | bytes 11409408 | tf_op jit(solution)/shard_map/dot_general | solution.py:34
  143.7 2.8 fusion.205
  146.5 2.0 fusion.198
  148.5 6.2 %fusion.105 = (f32[384]{0:T(512)S(1)}, f32[384]{0:T(512)}, f32[384]{0:T(512)}, f32[384]{0:T(512)}, f32[384]{0:T(512)}, /*index=5*/f32[384]{0:T(512)}, f32[384]{0...) fusion(bf16[4,16,16,384]{3,2,1,0:T(8,128)(2,1)S(1)} %bitcast.16, ...), kind=kLoop, calls=%fused_computation.306 | loop fusion | flops 23586048 | bytes 5549056 | tf_op jit(solution)/shard_map/reduce_sum | solution.py:134
  154.7 2.6 fusion.104
  157.3 3.8 %fusion.106 = (f32[384]{0:T(512)S(1)}, f32[384]{0:T(512)S(1)}, f32[384]{0:T(512)S(1)}, f32[384]{0:T(512)S(1)}, f32[384]{0:T(512)S(1)}, /*index=5*/f32[384]{0:T(5...) fusion(bf16[4,16,16,384]{3,2,1,0:T(8,128)(2,1)S(1)} %bitcast.16, ...), kind=kLoop, calls=%fused_computation.307 | loop fusion | flops 21226752 | bytes 2386944 | tf_op jit(solution)/shard_map/reduce_sum | solution.py:134
  161.1 3.2 reshape.389
  164.4 3.2 reshape.390
  169.1 1.1 copy-done.2
  170.2 1.0 broadcast_select_fusion
  171.8 149.4 %all-reduce.10.cloned.1.call-done = (f32[589824]{0:T(1024)}, f32[589824]{0:T(1024)}, f32[18816]{0:T(1024)}) async-done(((f32[589824]{0:T(1024)}, f32[589824]{0:T(1024)}, f32[18816]{0:T(1024)}), (f32[589824]{0:T(1024)}, f32[589824]{0:T(1024)}, f32[18816]{0:T(1024)})) %all-reduce.10.cloned.1.call-update) | async-done | bytes 4793872
  321.3 1.4 dynamic-slice.1
  322.7 1.4 dynamic-slice.2
  324.1 1.3 dynamic-slice.3
  (260 shorter events, 14.2 us)
Async XLA Ops:
  7.2 56.2 %copy-start = (bf16[384,1536]{1,0:T(8,128)(2,1)S(1)}, bf16[384,1536]{1,0:T(8,128)(2,1)}, u32[]{:S(2)}) copy-start(bf16[384,1536]{1,0:T(8,128)(2,1)} %param.26) | copy-start | bytes 3538948
  8.1 2.3 copy-start.47
  12.4 6.1 %copy-start.70 = (s32[8,1,8]{2,1,0:T(1,128)S(1)}, s32[8,1,8]{2,1,0:T(1,128)}, u32[]{:S(2)}) copy-start(s32[8,1,8]{2,1,0:T(1,128)} %param.21) | copy-start | bytes 772
  12.4 9.3 %copy-start.3 = (f32[49,384]{1,0:T(8,128)S(1)}, f32[49,384]{1,0:T(8,128)}, u32[]{:S(2)}) copy-start(f32[49,384]{1,0:T(8,128)} %param.22) | copy-start | bytes 225796
  12.4 12.0 %copy-start.73 = (s32[2,8]{1,0:T(2,128)S(1)}, s32[2,8]{1,0:T(2,128)}, u32[]{:S(2)}) copy-start(s32[2,8]{1,0:T(2,128)} %param.19) | copy-start | bytes 196
  12.4 26.8 %all-to-all-start = ((bf16[8,16,16,384]{3,2,1,0:T(8,128)(2,1)}), bf16[8,16,16,384]{3,2,1,0:T(8,128)(2,1)S(1)}, u32[]{:S(2)}, u32[]{:S(2)}) async-start(bf16[8,16,16,384]{3,2,1,0:T(8,128)(2,1)} %copy.34), calls=%async_computation | async-start | bytes 3145728 | tf_op jit(solution)/shard_map/all_to_all | solution.py:254
  24.4 15.8 %copy-start.67 = (pred[4,8]{1,0:T(4,128)(4,1)}, pred[4,8]{1,0:T(4,128)(4,1)S(1)}, u32[]{:S(2)}) copy-start(pred[4,8]{1,0:T(4,128)(4,1)S(1)} %get-tuple-element.121) | copy-start | bytes 100
  42.6 0.7 copy-start.39
  42.6 0.7 copy-start.40
  63.4 5.5 %copy-start.77 = (bf16[384,768]{1,0:T(8,128)(2,1)S(1)}, bf16[384,768]{1,0:T(8,128)(2,1)}, u32[]{:S(2)}) copy-start(bf16[384,768]{1,0:T(8,128)(2,1)} %param.31) | copy-start | bytes 1769476
  68.9 1.4 copy-start.1
  68.9 1.4 copy-start.68
  68.9 7.6 %copy-start.71 = (f32[1,768]{1,0:T(1,128)S(1)}, f32[1,768]{1,0:T(1,128)}, u32[]{:S(2)}) copy-start(f32[1,768]{1,0:T(1,128)} %param.35) | copy-start | bytes 9220
  68.9 12.2 %copy-start.44 = (f32[8,384]{1,0:T(8,128)S(1)}, f32[8,384]{1,0:T(8,128)}, u32[]{:S(2)}) copy-start(f32[8,384]{1,0:T(8,128)} %get-tuple-element.129) | copy-start | bytes 36868
  68.9 12.2 %copy-start.45 = (f32[8,384]{1,0:T(8,128)S(1)}, f32[8,384]{1,0:T(8,128)}, u32[]{:S(2)}) copy-start(f32[8,384]{1,0:T(8,128)} %get-tuple-element.130) | copy-start | bytes 36868
  68.9 12.2 %copy-start.48 = (pred[8,8]{1,0:T(8,128)(4,1)S(1)}, pred[8,8]{1,0:T(8,128)(4,1)}, u32[]{:S(2)}) copy-start(pred[8,8]{1,0:T(8,128)(4,1)} %copy-done.47) | copy-start | bytes 196
  69.0 20.7 %copy-start.4 = (f32[7,768]{1,0:T(8,128)S(1)}, f32[7,768]{1,0:T(8,128)}, u32[]{:S(2)}) copy-start(f32[7,768]{1,0:T(8,128)} %param.32) | copy-start | bytes 64516
  70.3 26.6 %copy-start.80 = (f32[768]{0:T(1024)S(1)}, f32[768]{0:T(1024)}, u32[]{:S(2)}) copy-start(f32[768]{0:T(1024)} %param.34) | copy-start | bytes 9220
  72.3 8.8 %all-to-all-start.1 = ((bf16[8,2,384]{2,1,0:T(2,128)(2,1)}), bf16[8,2,384]{2,1,0:T(2,128)(2,1)S(1)}, u32[]{:S(2)}, u32[]{:S(2)}) async-start(bf16[8,2,384]{2,1,0:T(2,128)(2,1)} %reshape.453), calls=%async_computation.1 | async-start | bytes 24576 | tf_op jit(solution)/shard_map/all_to_all | solution.py:262
  82.0 14.7 %all-to-all-start.2 = ((bf16[16,8,1,768]{3,1,2,0:T(8,128)(2,1)}), bf16[16,8,1,768]{3,1,2,0:T(8,128)(2,1)S(1)}, u32[]{:S(2)}, u32[]{:S(2)}) async-start(bf16[16,8,1,768]{3,1,2,0:T(8,128)(2,1)} %stack.153), calls=%async_computation.2 | async-start | bytes 393216 | tf_op jit(solution)/shard_map/all_to_all | solution.py:274
  89.6 231.6 %all-reduce.10.cloned.1.call-start = ((), (), s32[]{:S(2)}) async-start(), calls=%async_computation.4 | async-start | bytes 9592832
  96.9 2.6 copy-start.75
  124.7 4.1 %copy-start.49 = (f32[384]{0:T(512)S(1)}, f32[384]{0:T(512)}, u32[]{:S(2)}) copy-start(f32[384]{0:T(512)} %param.25) | copy-start | bytes 4612
  124.7 4.0 %copy-start.50 = (f32[384]{0:T(512)S(1)}, f32[384]{0:T(512)}, u32[]{:S(2)}) copy-start(f32[384]{0:T(512)} %param.24) | copy-start | bytes 4612
  129.5 2.7 copy-start.76
  129.5 2.7 copy-start.81
  129.5 2.7 copy-start.82
  132.2 1.9 copy-start.46
  132.2 1.9 copy-start.78
  164.2 3.5 %copy-start.66 = (f32[384]{0:T(512)S(1)}, f32[384]{0:T(512)}, u32[]{:S(2)}) copy-start(f32[384]{0:T(512)} %get-tuple-element.26) | copy-start | bytes 4612
  164.2 3.6 %copy-start.65 = (f32[384]{0:T(512)S(1)}, f32[384]{0:T(512)}, u32[]{:S(2)}) copy-start(f32[384]{0:T(512)} %get-tuple-element.27) | copy-start | bytes 4612
  164.2 3.6 %copy-start.64 = (f32[384]{0:T(512)S(1)}, f32[384]{0:T(512)}, u32[]{:S(2)}) copy-start(f32[384]{0:T(512)} %get-tuple-element.28) | copy-start | bytes 4612
  164.2 3.6 %copy-start.63 = (f32[384]{0:T(512)S(1)}, f32[384]{0:T(512)}, u32[]{:S(2)}) copy-start(f32[384]{0:T(512)} %get-tuple-element.29) | copy-start | bytes 4612
  164.2 3.6 %copy-start.62 = (f32[384]{0:T(512)S(1)}, f32[384]{0:T(512)}, u32[]{:S(2)}) copy-start(f32[384]{0:T(512)} %get-tuple-element.30) | copy-start | bytes 4612
  164.2 3.6 %copy-start.61 = (f32[384]{0:T(512)S(1)}, f32[384]{0:T(512)}, u32[]{:S(2)}) copy-start(f32[384]{0:T(512)} %get-tuple-element.31) | copy-start | bytes 4612
  164.3 3.6 %copy-start.60 = (f32[384]{0:T(512)S(1)}, f32[384]{0:T(512)}, u32[]{:S(2)}) copy-start(f32[384]{0:T(512)} %get-tuple-element.32) | copy-start | bytes 4612
  164.3 3.7 %copy-start.59 = (f32[384]{0:T(512)S(1)}, f32[384]{0:T(512)}, u32[]{:S(2)}) copy-start(f32[384]{0:T(512)} %get-tuple-element.33) | copy-start | bytes 4612
  164.3 3.7 %copy-start.58 = (f32[384]{0:T(512)S(1)}, f32[384]{0:T(512)}, u32[]{:S(2)}) copy-start(f32[384]{0:T(512)} %get-tuple-element.34) | copy-start | bytes 4612
  164.3 3.7 %copy-start.57 = (f32[384]{0:T(512)S(1)}, f32[384]{0:T(512)}, u32[]{:S(2)}) copy-start(f32[384]{0:T(512)} %get-tuple-element.35) | copy-start | bytes 4612
  164.3 3.7 %copy-start.56 = (f32[384]{0:T(512)S(1)}, f32[384]{0:T(512)}, u32[]{:S(2)}) copy-start(f32[384]{0:T(512)} %get-tuple-element.36) | copy-start | bytes 4612
  164.3 3.7 %copy-start.55 = (f32[384]{0:T(512)S(1)}, f32[384]{0:T(512)}, u32[]{:S(2)}) copy-start(f32[384]{0:T(512)} %get-tuple-element.37) | copy-start | bytes 4612
  164.3 3.7 %copy-start.54 = (f32[384]{0:T(512)S(1)}, f32[384]{0:T(512)}, u32[]{:S(2)}) copy-start(f32[384]{0:T(512)} %get-tuple-element.38) | copy-start | bytes 4612
  164.3 3.7 %copy-start.53 = (f32[384]{0:T(512)S(1)}, f32[384]{0:T(512)}, u32[]{:S(2)}) copy-start(f32[384]{0:T(512)} %get-tuple-element.39) | copy-start | bytes 4612
  164.3 3.7 %copy-start.52 = (f32[384]{0:T(512)S(1)}, f32[384]{0:T(512)}, u32[]{:S(2)}) copy-start(f32[384]{0:T(512)} %get-tuple-element.40) | copy-start | bytes 4612
  164.3 3.7 %copy-start.51 = (f32[384]{0:T(512)S(1)}, f32[384]{0:T(512)}, u32[]{:S(2)}) copy-start(f32[384]{0:T(512)} %get-tuple-element.41) | copy-start | bytes 4612
  169.1 1.1 copy-start.2
  169.1 1.1 copy-start.72
  169.1 2.1 copy-start.69
  (39 other events, 26.6 us)
Sparse Core Ops, SparseCore 0:
  169.2 151.9 all-reduce.9
